TPU v7x, 128 devices: a whole 4x4x4 slice. The times are simulated.
128 devices in a mesh: vox: 32 (over z, y, core), ray: 4 (over x).
Axes of the slice: x: 4, y: 4, z: 4, core: 2. Of those that a mesh axis runs over, the one named last changes fastest.
Arguments:
- weights: bfloat16 [1024, 4, 16, 128, 128], P('vox', 'ray'), may hold values from -0.5 to 0.5
- slot_block: int32 [1024, 4, 16], P('vox', 'ray'), may hold values from 0 to 1023
- slot_tile: int32 [1024, 4, 16], P('vox', 'ray'), may hold values from 0 to 63
- slot_count: int32 [1024, 4], P('vox', 'ray'), may hold values from 1 to 16, as said below
- observed: bfloat16 [2048, 4, 128], P('vox', 'ray'), may hold values from -6 to 6
- prior_scale: float32 [32, 128, 1024], P(None, 'vox'), may hold values from 0.2 to 1
Outputs:
- solution: float32 [32, 128, 1024], P(None, 'vox')
- residual: float32 [32, 128, 1024], P(None, 'vox')
Inputs may be any that keep to these rules, and one draw needn't show every extreme that they name: `slot_count`: live slots of one bucket, always the first ones; each device has a bucket holding its own largest count, and some bucket of some device holds 16.
All inputs are finite; a program needn't handle non-finite values.
Results may differ from a plain program's by a relative error of at most 0.0059.
Values may be sent and summed in bfloat16 or wider, within the bound.
A program may use at most 64 MiB of HBM per device.

v0:
```python
import jax
import jax.numpy as jnp
from jax import lax
from jax.sharding import PartitionSpec as P

ITERS = 2


def padded_2(block, sides, width):
    for axis, dim in sides:
        count = lax.axis_size(axis)
        forward = [(i, i + 1) for i in range(count - 1)]
        backward = [(target, source) for source, target in forward]
        low = lax.ppermute(
            lax.slice_in_dim(block, block.shape[dim] - width, None, axis=dim), axis, forward
        )
        high = lax.ppermute(lax.slice_in_dim(block, 0, width, axis=dim), axis, backward)
        block = jnp.concatenate([low, block, high], axis=dim)
    return block


def on_device(weights, slot_block, slot_tile, slot_count, observed, prior_scale):
    highest = lax.Precision.HIGHEST
    levels, columns, across = prior_scale.shape
    slot_total = weights.shape[2]
    block_len = weights.shape[4]
    tile_total = observed.shape[0]
    block_total = levels * columns * across // block_len
    tile_weights = weights[:, 0]
    block_ids = slot_block[:, 0]
    tile_ids = slot_tile[:, 0]
    live_mask = (jnp.arange(slot_total)[None, :] < slot_count[:, 0][:, None]).astype(jnp.float32)
    tile_onehot = (tile_ids[:, :, None] == jnp.arange(tile_total)[None, None, :]).astype(
        jnp.float32
    )
    wanted = lax.all_to_all(block_ids, "vox", split_axis=0, concat_axis=0, tiled=True)
    wanted_flat = wanted.reshape(-1)

    def place(rows, targets):
        return jnp.zeros((block_total, block_len), jnp.float32).at[targets].add(rows)

    def forward(direction_low):
        picked = jnp.take(direction_low, wanted, axis=0)
        fetched = lax.all_to_all(picked, "vox", split_axis=0, concat_axis=0, tiled=True)
        ray_part = jnp.einsum(
            "ustb,usb->ust", tile_weights, fetched, preferred_element_type=jnp.float32
        )
        ray_part = ray_part * live_mask[:, :, None]
        ray_sums = jnp.einsum("usk,ust->kt", tile_onehot, ray_part, precision=highest)
        return ray_sums

    def transposed(ray_values):
        ray_rows = jnp.take(ray_values, tile_ids, axis=0)
        voxel_part = jnp.einsum(
            "ustb,ust->usb", tile_weights, ray_rows, preferred_element_type=jnp.float32
        )
        voxel_part = voxel_part * live_mask[:, :, None]
        returned = lax.all_to_all(voxel_part, "vox", split_axis=0, concat_axis=0, tiled=True)
        return returned.reshape(-1, block_len)

    def combine(used_part):
        grouped = lax.psum(place(used_part, wanted_flat), "ray")
        return grouped

    initial = combine(transposed(observed[:, 0]))

    def squares_here(vector):
        return lax.psum(jnp.sum(vector * vector), "vox")

    residual = initial
    solution = jnp.zeros_like(residual)
    direction = residual
    norm_now = squares_here(residual)
    for iteration in range(ITERS):
        scaled = prior_scale * direction.reshape(levels, columns, across)
        with_faces = padded_2(scaled, (("vox", 1),), 1)
        padded = jnp.pad(with_faces, ((1, 1), (0, 0), (1, 1)))
        beside = padded[2:, 1:-1, 1:-1] + padded[:-2, 1:-1, 1:-1]
        beside = beside + padded[1:-1, 2:, 1:-1] + padded[1:-1, :-2, 1:-1]
        beside = beside + padded[1:-1, 1:-1, 2:] + padded[1:-1, 1:-1, :-2]
        normal_ray_values = forward(direction.astype(jnp.bfloat16)).astype(jnp.bfloat16)
        curved = combine(transposed(normal_ray_values)) + (
            prior_scale * (6.0 * scaled - beside)
        ).reshape(block_total, block_len)
        step_size = norm_now / lax.psum(jnp.sum(direction * curved), "vox")
        solution = solution + step_size * direction
        residual = residual - step_size * curved
        norm_next = squares_here(residual)
        direction = residual + norm_next / norm_now * direction
        norm_now = norm_next
    solution, residual = (solution, residual)
    return (solution.reshape(levels, columns, across), residual.reshape(levels, columns, across))


def solution(mesh):
    in_specs = (
        P("vox", "ray", None, None, None),
        P("vox", "ray", None),
        P("vox", "ray", None),
        P("vox", "ray"),
        P("vox", "ray", None),
        P(None, "vox", None),
    )
    out_specs = (P(None, "vox", None), P(None, "vox", None))
    return jax.shard_map(
        on_device, mesh=mesh, in_specs=in_specs, out_specs=out_specs, check_vma=False
    )
```

profile of v0, /device:TPU:1, one launch (start us, length us, event | category | flops | bytes accessed | tf_op | source)
XLA Modules:
  0.0 493.0 jit_solution(16306785719110435040)
XLA Ops:
  7.2 1.4 copy.30
  8.6 9.6 %all-to-all-start = ((s32[32,1,16]{2,1,0:T(1,128)}), s32[32,1,16]{2,1,0:T(1,128)S(1)}, u32[]{:S(2)}, u32[]{:S(2)}) async-start(s32[32,1,16]{2,1,0:T(1,128)} %copy.30), calls=%async_computation | async-start | bytes 32768 | tf_op jit(solution)/shard_map/all_to_all | solution.py:36
  18.2 0.7 compare_select_fusion.1
  18.9 0.7 compare_and_fusion.1
  19.8 0.7 fusion.38
  20.6 1.3 gather_fusion
  22.1 8.0 %fusion.8 = f32[32,16,1,128]{3,2,1,0:T(1,128)S(1)} fusion(bf16[32,1,16,128,128]{4,3,2,1,0:T(8,128)(2,1)} %param.10, bf16[32,16,128,1]{2,1,0,3:T(8,128)(2,1)S(1)} %select_bitcast_fusion.2), kind=kOutput, calls=%fused_computation.16 | convolution fusion | flops 16777216 | bytes 17170432 | tf_op jit(solution)/shard_map/ustb,ust->usb/dot_general | solution.py:54
  30.1 0.9 broadcast_multiply_fusion.4
  31.0 7.4 %all-to-all-start.1 = ((f32[32,16,128]{2,1,0:T(8,128)}), f32[32,16,128]{2,1,0:T(8,128)S(1)}, u32[]{:S(2)}, u32[]{:S(2)}) async-start(f32[32,16,128]{2,1,0:T(8,128)} %broadcast_multiply_fusion.4), calls=%async_computation.1 | async-start | bytes 524288 | tf_op jit(solution)/shard_map/all_to_all | solution.py:58
  38.4 0.5 broadcast.125
  38.9 0.7 reduce.3
  39.7 7.6 %all-to-all-done.1 = f32[32,16,128]{2,1,0:T(8,128)S(1)} async-done(((f32[32,16,128]{2,1,0:T(8,128)}), f32[32,16,128]{2,1,0:T(8,128)S(1)}, u32[]{:S(2)}, u32[]{:S(2)}) %all-to-all-start.1) | async-done | bytes 262176 | tf_op jit(solution)/shard_map/all_to_all | solution.py:58
  47.2 3.0 scatter_custom_fusion
  50.4 38.3 %all-reduce.7.cloned.1.call-done = f32[1024,128]{1,0:T(8,128)} async-done(((f32[1024,128]{1,0:T(8,128)}), f32[1024,128]{1,0:T(8,128)}) %all-reduce.7.cloned.1.call-update) | async-done | bytes 524304 | tf_op jit(solution)/shard_map/psum | solution.py:62
  88.7 1.1 convert_element_type.24
  89.9 1.3 gather_fusion.1
  91.2 0.8 broadcast_select_fusion.1
  92.0 9.7 %all-to-all-start.2 = ((bf16[32,16,128]{2,1,0:T(8,128)(2,1)}), bf16[32,16,128]{2,1,0:T(8,128)(2,1)S(1)}, u32[]{:S(2)}, u32[]{:S(2)}) async-start(bf16[32,16,128]{2,1,0:T(8,128)(2,1)} %broadcast_select_fusion.1), calls=%async_computation.2 | async-start | bytes 262144 | tf_op jit(solution)/shard_map/all_to_all | solution.py:44
  101.7 0.2 reshape.103
  102.1 7.3 %all-to-all-done.2 = bf16[32,16,128]{2,1,0:T(8,128)(2,1)S(1)} async-done(((bf16[32,16,128]{2,1,0:T(8,128)(2,1)}), bf16[32,16,128]{2,1,0:T(8,128)(2,1)S(1)}, u32[]{:S(2)}, u32[]{:S(2)}) %all-to-all-start.2) | async-done | bytes 131104 | tf_op jit(solution)/shard_map/all_to_all | solution.py:44
  109.4 12.2 %fusion.6 = f32[32,16,1,128]{3,2,1,0:T(1,128)S(1)} fusion(bf16[32,1,16,128,128]{4,3,2,1,0:T(8,128)(2,1)} %param.10, bf16[32,16,128,1]{2,1,0,3:T(8,128)(2,1)S(1)} %bitcast.55), kind=kOutput, calls=%fused_computation.14 | convolution fusion | flops 16777216 | bytes 17170432 | tf_op jit(solution)/shard_map/ustb,usb->ust/dot_general | solution.py:45
  121.6 0.2 broadcast_multiply_fusion.3
  121.8 0.5 fusion.13
  122.3 1.3 gather_fusion.2
  123.8 8.0 %fusion.4 = f32[32,16,1,128]{3,2,1,0:T(1,128)S(1)} fusion(bf16[32,1,16,128,128]{4,3,2,1,0:T(8,128)(2,1)} %param.10, bf16[32,16,128,1]{2,1,0,3:T(8,128)(2,1)S(1)} %select_bitcast_fusion.1), kind=kOutput, calls=%fused_computation.12 | convolution fusion | flops 16777216 | bytes 17170432 | tf_op jit(solution)/shard_map/ustb,ust->usb/dot_general | solution.py:54
  131.8 0.9 broadcast_multiply_fusion.2
  132.7 3.9 all-to-all-start.3
  136.6 0.2 fusion.41
  136.9 3.5 collective-permute-start
  140.4 2.1 collective-permute-start.1
  142.5 3.1 all-to-all-done.3
  145.6 3.0 scatter_custom_fusion.1
  148.7 1.1 select_maximum_fusion.2
  149.8 1.0 fusion.20
  150.8 0.2 reshape.104
  151.0 36.2 %all-reduce.9.cloned.1.call-done = f32[1024,128]{1,0:T(8,128)} async-done(((f32[1024,128]{1,0:T(8,128)}), f32[1024,128]{1,0:T(8,128)}) %all-reduce.9.cloned.1.call-update) | async-done | bytes 524304 | tf_op jit(solution)/shard_map/psum | solution.py:62
  187.2 1.8 multiply_reduce_fusion.2
  189.0 65.5 %all-reduce.2 = (f32[]{:T(128)}, f32[]{:T(128)}) all-reduce(f32[]{:T(128)} %get-tuple-element.5, f32[]{:T(128)} %get-tuple-element.4), channel_id=1, replica_groups=mesh['vox'=32,'ray'=4] {'vox'}, use_global_device_ids=true, to_apply=%region_3.5 | all-reduce | flops 2 | bytes 16 | tf_op jit(solution)/shard_map/psum | solution.py:68
  255.8 0.7 multiply_reduce_fusion.1
  256.6 65.7 %psum.53 = f32[]{:T(128)} all-reduce(f32[]{:T(128)} %multiply_reduce_fusion.1), channel_id=1, replica_groups=mesh['vox'=32,'ray'=4] {'vox'}, use_global_device_ids=true, to_apply=%region_9.12 | all-reduce | flops 1 | bytes 8 | tf_op jit(solution)/shard_map/psum | solution.py:68
  323.8 1.3 gather_fusion.3
  325.2 0.8 broadcast_select_fusion
  326.0 4.2 all-to-all-start.4
  330.1 0.2 reshape.106
  330.5 7.4 %all-to-all-done.4 = bf16[32,16,128]{2,1,0:T(8,128)(2,1)S(1)} async-done(((bf16[32,16,128]{2,1,0:T(8,128)(2,1)}), bf16[32,16,128]{2,1,0:T(8,128)(2,1)S(1)}, u32[]{:S(2)}, u32[]{:S(2)}) %all-to-all-start.4) | async-done | bytes 131104 | tf_op jit(solution)/shard_map/all_to_all | solution.py:44
  337.9 12.2 %fusion.2 = f32[32,16,1,128]{3,2,1,0:T(1,128)S(1)} fusion(bf16[32,1,16,128,128]{4,3,2,1,0:T(8,128)(2,1)} %param.10, bf16[32,16,128,1]{2,1,0,3:T(8,128)(2,1)S(1)} %bitcast.54), kind=kOutput, calls=%fused_computation.10 | convolution fusion | flops 16777216 | bytes 17170432 | tf_op jit(solution)/shard_map/ustb,usb->ust/dot_general | solution.py:45
  350.2 0.5 fusion.14
  350.7 1.3 gather_fusion.4
  352.2 8.0 %fusion = f32[32,16,1,128]{3,2,1,0:T(1,128)S(1)} fusion(bf16[32,1,16,128,128]{4,3,2,1,0:T(8,128)(2,1)} %param.10, bf16[32,16,128,1]{2,1,0,3:T(8,128)(2,1)S(1)} %select_bitcast_fusion), kind=kOutput, calls=%fused_computation.8 | convolution fusion | flops 16777216 | bytes 17170432 | tf_op jit(solution)/shard_map/ustb,ust->usb/dot_general | solution.py:54
  360.3 0.9 broadcast_multiply_fusion
  361.1 3.9 all-to-all-start.5
  365.1 0.2 fusion.40
  365.3 3.5 collective-permute-start.2
  368.9 2.1 collective-permute-start.3
  371.0 3.0 all-to-all-done.5
  374.1 3.0 scatter_custom_fusion.2
  377.1 1.1 select_maximum_fusion
  378.3 1.0 fusion.16
  379.3 0.2 reshape.107
  379.5 36.2 %all-reduce.11.cloned.1.call-done = f32[1024,128]{1,0:T(8,128)} async-done(((f32[1024,128]{1,0:T(8,128)}), f32[1024,128]{1,0:T(8,128)}) %all-reduce.11.cloned.1.call-update) | async-done | bytes 524304 | tf_op jit(solution)/shard_map/psum | solution.py:62
  415.7 1.8 multiply_reduce_fusion
  417.5 65.5 %psum.55 = f32[]{:T(128)} all-reduce(f32[]{:T(128)} %get-tuple-element.8), channel_id=1, replica_groups=mesh['vox'=32,'ray'=4] {'vox'}, use_global_device_ids=true, to_apply=%region_13.16 | all-reduce | flops 1 | bytes 8 | tf_op jit(solution)/shard_map/psum | solution.py:85
  484.5 1.0 reshape.108
  485.5 1.0 reshape.109
  (37 shorter events, 1.8 us)
Async XLA Ops:
  7.2 13.4 %copy-start = (bf16[64,1,128]{2,0,1:T(8,128)(2,1)S(1)}, bf16[64,1,128]{2,0,1:T(8,128)(2,1)}, u32[]{:S(2)}) copy-start(bf16[64,1,128]{2,0,1:T(8,128)(2,1)} %param.14) | copy-start | bytes 49156
  8.6 22.4 %all-to-all-start = ((s32[32,1,16]{2,1,0:T(1,128)}), s32[32,1,16]{2,1,0:T(1,128)S(1)}, u32[]{:S(2)}, u32[]{:S(2)}) async-start(s32[32,1,16]{2,1,0:T(1,128)} %copy.30), calls=%async_computation | async-start | bytes 32768 | tf_op jit(solution)/shard_map/all_to_all | solution.py:36
  31.0 16.3 %all-to-all-start.1 = ((f32[32,16,128]{2,1,0:T(8,128)}), f32[32,16,128]{2,1,0:T(8,128)S(1)}, u32[]{:S(2)}, u32[]{:S(2)}) async-start(f32[32,16,128]{2,1,0:T(8,128)} %broadcast_multiply_fusion.4), calls=%async_computation.1 | async-start | bytes 524288 | tf_op jit(solution)/shard_map/all_to_all | solution.py:58
  38.3 50.4 %all-reduce.7.cloned.1.call-start = ((), (), s32[]{:S(2)}) async-start(), calls=%async_computation.6 | async-start | bytes 1048576 | tf_op jit(solution)/shard_map/psum | solution.py:62
  88.7 13.0 %copy-start.1 = (f32[1024,128]{1,0:T(8,128)S(1)}, f32[1024,128]{1,0:T(8,128)}, u32[]{:S(2)}) copy-start(f32[1024,128]{1,0:T(8,128)} %all-reduce.7.cloned.1.call-done) | copy-start | bytes 1572868
  89.9 12.1 %copy-start.2 = (f32[32,4,1024]{2,1,0:T(4,128)S(1)}, f32[32,4,1024]{2,1,0:T(4,128)}, u32[]{:S(2)}) copy-start(f32[32,4,1024]{2,1,0:T(4,128)} %param.15) | copy-start | bytes 1572868
  92.0 17.3 %all-to-all-start.2 = ((bf16[32,16,128]{2,1,0:T(8,128)(2,1)}), bf16[32,16,128]{2,1,0:T(8,128)(2,1)S(1)}, u32[]{:S(2)}, u32[]{:S(2)}) async-start(bf16[32,16,128]{2,1,0:T(8,128)(2,1)} %broadcast_select_fusion.1), calls=%async_computation.2 | async-start | bytes 262144 | tf_op jit(solution)/shard_map/all_to_all | solution.py:44
  109.4 12.4 %copy-start.3 = (s32[32,1,16]{0,2,1:T(8,128)S(1)}, s32[32,1,16]{0,2,1:T(8,128)}, u32[]{:S(2)}) copy-start(s32[32,1,16]{0,2,1:T(8,128)} %param.12) | copy-start | bytes 6148
  132.7 12.9 %all-to-all-start.3 = ((f32[32,16,128]{2,1,0:T(8,128)}), f32[32,16,128]{2,1,0:T(8,128)S(1)}, u32[]{:S(2)}, u32[]{:S(2)}) async-start(f32[32,16,128]{2,1,0:T(8,128)} %broadcast_multiply_fusion.2), calls=%async_computation.3 | async-start | bytes 524288 | tf_op jit(solution)/shard_map/all_to_all | solution.py:58
  136.6 50.6 %all-reduce.9.cloned.1.call-start = ((), (), s32[]{:S(2)}) async-start(), calls=%async_computation.7 | async-start | bytes 1048576 | tf_op jit(solution)/shard_map/psum | solution.py:62
  136.9 11.8 %collective-permute-start = (f32[32,1,1024]{2,1,0:T(1,128)S(1)}, f32[32,1,1024]{2,1,0:T(1,128)S(1)}, u32[]{:S(2)}, u32[]{:S(2)}) collective-permute-start(f32[32,1,1024]{2,1,0:T(1,128)S(1)} %get-tuple-element.17), channel_id=1, source_target_pairs={{0,4},{4,8},{8,12},{12,16},{16,20},{20,24},{24,28},{28,32},{32,36}... | collective-permute-start | bytes 393224 | tf_op jit(solution)/shard_map/ppermute | solution.py:14
  140.4 8.3 %collective-permute-start.1 = (f32[32,1,1024]{2,1,0:T(1,128)S(1)}, f32[32,1,1024]{2,1,0:T(1,128)S(1)}, u32[]{:S(2)}, u32[]{:S(2)}) collective-permute-start(f32[32,1,1024]{2,1,0:T(1,128)S(1)} %get-tuple-element.18), channel_id=1, source_target_pairs={{4,0},{8,4},{12,8},{16,12},{20,16},{24,20},{28,24},{32,28},{36,32}... | collective-permute-start | bytes 393224 | tf_op jit(solution)/shard_map/ppermute | solution.py:17
  326.0 11.9 %all-to-all-start.4 = ((bf16[32,16,128]{2,1,0:T(8,128)(2,1)}), bf16[32,16,128]{2,1,0:T(8,128)(2,1)S(1)}, u32[]{:S(2)}, u32[]{:S(2)}) async-start(bf16[32,16,128]{2,1,0:T(8,128)(2,1)} %broadcast_select_fusion), calls=%async_computation.4 | async-start | bytes 262144 | tf_op jit(solution)/shard_map/all_to_all | solution.py:44
  361.1 12.9 %all-to-all-start.5 = ((f32[32,16,128]{2,1,0:T(8,128)}), f32[32,16,128]{2,1,0:T(8,128)S(1)}, u32[]{:S(2)}, u32[]{:S(2)}) async-start(f32[32,16,128]{2,1,0:T(8,128)} %broadcast_multiply_fusion), calls=%async_computation.5 | async-start | bytes 524288 | tf_op jit(solution)/shard_map/all_to_all | solution.py:58
  365.1 50.6 %all-reduce.11.cloned.1.call-start = ((), (), s32[]{:S(2)}) async-start(), calls=%async_computation.8 | async-start | bytes 1048576 | tf_op jit(solution)/shard_map/psum | solution.py:62
  365.3 11.8 %collective-permute-start.2 = (f32[32,1,1024]{2,1,0:T(1,128)S(1)}, f32[32,1,1024]{2,1,0:T(1,128)S(1)}, u32[]{:S(2)}, u32[]{:S(2)}) collective-permute-start(f32[32,1,1024]{2,1,0:T(1,128)S(1)} %get-tuple-element.15), channel_id=1, source_target_pairs={{0,4},{4,8},{8,12},{12,16},{16,20},{20,24},{24,28},{28,32},{32,36}... | collective-permute-start | bytes 393224 | tf_op jit(solution)/shard_map/ppermute | solution.py:14
  368.9 8.3 %collective-permute-start.3 = (f32[32,1,1024]{2,1,0:T(1,128)S(1)}, f32[32,1,1024]{2,1,0:T(1,128)S(1)}, u32[]{:S(2)}, u32[]{:S(2)}) collective-permute-start(f32[32,1,1024]{2,1,0:T(1,128)S(1)} %get-tuple-element.16), channel_id=1, source_target_pairs={{4,0},{8,4},{12,8},{16,12},{20,16},{24,20},{28,24},{32,28},{36,32}... | collective-permute-start | bytes 393224 | tf_op jit(solution)/shard_map/ppermute | solution.py:17
Sparse Core Ops, SparseCore 0:
  50.4 38.2 all-reduce.6
  148.8 38.3 all-reduce.8
  377.2 38.4 all-reduce.10
where the time goes:
time: 496 us; the launch traced here: 493 us
  blocking collectives  197 us (40%)
  waiting for transfers between devices  139 us (28%)
  starting transfers between devices  50.2 us (10%)
  matrix products  49.6 us (10%)
  other arithmetic  27.1 us (5%)
  between operations  18.2 us (4%)
  local copies, waits for them, and re-layouts  12.1 us (2%)
    psum x2, blocking collectives, squares_here(): return lax.psum(jnp.sum(vector * vector), 'vox')  131 us
    psum x3, waiting for transfers between devices, combine(): grouped = lax.psum(place(used_part, wanted_flat), 'ray')  111 us
    psum x1, blocking collectives, on_device(): step_size = norm_now / lax.psum(jnp.sum(direction * curved), 'vox')  65.5 us
    dot_general x2, matrix products, forward(): jnp.einsum('ustb,usb->ust', tile_weights, fetched, preferred_element_type...  24.5 us
    dot_general x3, matrix products, transposed(): jnp.einsum('ustb,ust->usb', tile_weights, ray_rows, preferred_element_typ...  24.1 us
    all_to_all x3, starting transfers between devices, transposed(): lax.all_to_all(voxel_part, 'vox', split_axis=0, concat_axis=0, tiled=True)  15.2 us
    all_to_all x2, waiting for transfers between devices, forward(): lax.all_to_all(picked, 'vox', split_axis=0, concat_axis=0, tiled=True)  14.6 us
    all_to_all x2, starting transfers between devices, forward(): lax.all_to_all(picked, 'vox', split_axis=0, concat_axis=0, tiled=True)  13.9 us
  transfers between devices with their start and end apart: 13, of which 8 were waited for; matrix products, arithmetic and copies ran while one was open for 5% of the time, Pallas kernels for 0%

commit v1 on v0

v1 whole, which is shorter than its diff:
```python
import functools

import jax
import jax.numpy as jnp
from jax import lax
from jax.experimental import pallas as pl
from jax.experimental.pallas import tpu as pltpu
from jax.sharding import PartitionSpec as P

F32 = jnp.float32
BF16 = jnp.bfloat16
MESH = pl.DeviceIdType.MESH
NT = (((1,), (1,)), ((), ()))


def dot(a, b):
    return jnp.dot(a, b, preferred_element_type=F32)


def dot_nt(a, b):
    return lax.dot_general(a, b, NT, preferred_element_type=F32)


def iota(shape, dim):
    return lax.broadcasted_iota(jnp.int32, shape, dim)


def halves(x):
    high = x.astype(BF16)
    return high, (x - high.astype(F32)).astype(BF16)


def block_transpose(a):
    which = lax.rem(iota(a.shape, 1) // 32 - iota(a.shape, 0) // 4 + 4, 4)
    out = a
    for step in range(1, 4):
        moved = pltpu.roll(pltpu.roll(a, 32 * step, 1), 16 - 4 * step, 0)
        out = jnp.where(which == step, moved, out)
    return out


def block_diagonal(rows):
    slots, length = rows.shape
    wide = jnp.concatenate([rows] * slots, axis=1)
    own = iota(wide.shape, 0) == iota(wide.shape, 1) // length
    return jnp.where(own, wide, jnp.zeros_like(wide))


def kernel(
    n_vox, n_ray, dims,
    w_hbm, block_ref, tile_ref, count_ref, observed_ref, prior_ref,
    solution_ref, residual_ref,
    w, onehot, tile_hot, tile_hot_t, ray_rows, ray_part, prior_t,
    id_send, id_recv, prod_send, prod_recv, pick_send, pick_recv,
    scalar_send, scalar_recv, state, halo_x, halo_y, full,
    w_sem, x_send, x_recv, near_send, near_recv, local_sem,
):
    levels, columns, runs, lanes = dims
    n_dev = n_vox * n_ray
    pairs = n_vox // 2
    blocks = levels * columns * runs
    vox = lax.axis_index("vox")
    ray = lax.axis_index("ray")
    me = vox * n_ray + ray

    def pair_at(p):
        return lax.rem(vox // 2 + 1 + p, pairs)

    def w_copy(p):
        at = pl.ds(2 * pair_at(p), 2)
        return pltpu.make_async_copy(w_hbm.at[at], w.at[at], w_sem.at[p])

    def start_w(p, carry):
        w_copy(p).start()
        return carry

    lax.fori_loop(0, pairs, start_w, 0)

    barrier = pltpu.get_barrier_semaphore()

    def target(k):
        t = lax.rem(me + k, n_dev)
        return t, t // n_ray, lax.rem(t, n_ray)

    def greet(k, carry):
        _, tv, tr = target(k)
        pl.semaphore_signal(barrier, 1, device_id=(tv, tr), device_id_type=MESH)
        return carry

    lax.fori_loop(1, n_dev, greet, 0)

    def rows4(index):
        return pl.ds(pl.multiple_of(index * 4, 4), 4)

    def send_tile(src, dst, phase, tv, tr):
        pltpu.make_async_remote_copy(
            src, dst.at[rows4(me)], x_send.at[phase], x_recv.at[phase],
            device_id=(tv, tr), device_id_type=MESH,
        ).start()

    def keep_tile(src, dst):
        copy = pltpu.make_async_copy(src, dst.at[rows4(me)], local_sem)
        copy.start()
        copy.wait()

    def await_tiles(dst, phase, sems, rows):
        part = dst.at[pl.ds(0, (n_dev - 1) * rows)]
        pltpu.make_async_copy(part, part, sems.at[phase]).wait()

    slots = tile_ref.shape[0]
    live = iota((slots, n_vox), 0) < count_ref[...]
    tiles_live = jnp.where(live, tile_ref[...], -1)
    ids = block_ref[...].astype(F32)
    lane = iota((slots, lanes), 1)
    for u in range(n_vox):
        at = pl.ds(u * slots, slots)
        hot = jnp.where(tiles_live[:, u : u + 1] == lane, 1.0, 0.0)
        tile_hot[at] = hot.astype(BF16)
        spread = jnp.broadcast_to(ids[:, u : u + 1], (slots, lanes))
        id_send[pl.ds(u * 4, 4)] = block_transpose(spread)[:4]

    pl.semaphore_wait(barrier, n_dev - 1)

    def send_ids(k, carry):
        _, tv, tr = target(k)
        send_tile(id_send.at[rows4(tv)], id_recv, 0, tv, tr)
        return carry

    lax.fori_loop(1, n_dev, send_ids, 0)
    keep_tile(id_send.at[rows4(vox)], id_recv)

    def transposed(phase, buffer, parts):
        def step(p, carry):
            if phase == 1:
                w_copy(p).wait()
            first = 2 * pair_at(p)
            left = []
            for u in (first, first + 1):
                rows = ray_rows[pl.ds(pl.multiple_of(u * slots, slots), slots)]
                for part in range(parts):
                    left.append(block_diagonal(rows[:, part * lanes : (part + 1) * lanes]))
            right = jnp.concatenate(
                [w[first].reshape(-1, lanes), w[first + 1].reshape(-1, lanes)], axis=1
            )
            made = dot(jnp.concatenate(left, axis=0), right)
            for side, u in enumerate((first, first + 1)):
                columns_of = slice(side * lanes, (side + 1) * lanes)
                base = side * parts * slots
                rows = made[base : base + slots, columns_of]
                for part in range(1, parts):
                    rows = rows + made[base + part * slots : base + (part + 1) * slots, columns_of]
                prod_send[buffer, pl.ds(pl.multiple_of(u * slots, slots), slots)] = (
                    block_transpose(rows)
                )
            for side, u in enumerate((first, first + 1)):
                for k in range(n_ray):
                    tr = lax.rem(ray + k, n_ray)
                    src = prod_send.at[buffer].at[rows4(u * n_ray + tr)]

                    @pl.when(u * n_ray + tr != me)
                    def _():
                        send_tile(src, prod_recv.at[buffer], phase, u, tr)

            return carry

        lax.fori_loop(0, pairs, step, 0)
        keep_tile(prod_send.at[buffer].at[rows4(me)], prod_recv.at[buffer])

    def place(phase, buffer):
        await_tiles(prod_recv.at[buffer], phase, x_recv, 4)
        turned = prod_recv[buffer].T
        rows = turned.shape[1]
        total = None
        for q in range(4):
            high, low = halves(turned[q * 32 : (q + 1) * 32])
            part = dot(
                jnp.concatenate([high, low], axis=0), onehot[q * rows : (q + 1) * rows]
            )
            total = part if total is None else total + part
        return total[:32] + total[32:]

    def gather(phase, buffer, values):
        high, low = halves(values)
        both = jnp.concatenate([high, low], axis=0)
        rows = n_dev * 4
        chunk = rows // 2
        for half in range(2):
            pieces = []
            for q in range(4):
                start = q * rows + half * chunk
                got = dot_nt(both, onehot[start : start + chunk])
                pieces.append(got[:32] + got[32:])
            pick_send[buffer, pl.ds(half * chunk, chunk)] = jnp.concatenate(pieces, axis=0).T

            def send(k, carry):
                t = half * (n_dev // 2) + lax.rem(me + k, n_dev // 2)

                @pl.when(t != me)
                def _():
                    send_tile(
                        pick_send.at[buffer].at[rows4(t)], pick_recv.at[buffer], phase,
                        t // n_ray, lax.rem(t, n_ray),
                    )

                return carry

            lax.fori_loop(0, n_dev // 2, send, 0)
        keep_tile(pick_send.at[buffer].at[rows4(me)], pick_recv.at[buffer])

    def forward(phase, buffer):
        await_tiles(pick_recv.at[buffer], phase, x_recv, 4)

        def step(p, carry):
            left = []
            for side in range(2):
                at = pl.ds(pl.multiple_of((2 * p + side) * slots, slots), slots)
                high, low = halves(block_transpose(pick_recv[buffer, at]))
                left += [block_diagonal(high), block_diagonal(low)]
            right = jnp.concatenate(
                [
                    jnp.concatenate([w[2 * p + side, s] for s in range(slots)], axis=1)
                    for side in range(2)
                ],
                axis=0,
            )
            made = dot_nt(jnp.concatenate(left, axis=0), right)
            for side in range(2):
                at = pl.ds(pl.multiple_of((2 * p + side) * slots, slots), slots)
                columns_of = slice(side * lanes, (side + 1) * lanes)
                for part in range(2):
                    base = (2 * side + part) * slots
                    ray_part[part, at] = made[base : base + slots, columns_of]
            return carry

        lax.fori_loop(0, pairs, step, 0)

        def tiles_of(part):
            values = ray_part[part]
            a, rest = halves(values)
            rest = values - a.astype(F32)
            b = rest.astype(BF16)
            c = (rest - b.astype(F32)).astype(BF16)
            return dot(tile_hot_t[...], a) + dot(tile_hot_t[...], b) + dot(tile_hot_t[...], c)

        return tiles_of(0), tiles_of(1)

    def send_scalars(turn, first, second):
        lane_row = iota((8, lanes), 1)
        scalar_send[turn] = jnp.where(lane_row == 0, first, jnp.where(lane_row == 1, second, 0.0))
        src = scalar_send.at[turn].at[pl.ds(0, 1)]
        dst = scalar_recv.at[turn].at[pl.ds(me, 1)]
        copy = pltpu.make_async_copy(src, dst, local_sem)
        copy.start()
        copy.wait()

        def send(k, carry):
            _, tv, tr = target(k)
            pltpu.make_async_remote_copy(
                src, dst, x_send.at[6 + turn], x_recv.at[6 + turn],
                device_id=(tv, tr), device_id_type=MESH,
            ).start()
            return carry

        lax.fori_loop(1, n_dev, send, 0)

    def await_scalars(turn):
        await_tiles(scalar_recv.at[turn], 6 + turn, x_recv, 1)
        totals = jnp.sum(scalar_recv[turn], axis=0, keepdims=True)
        lane_row = iota((1, lanes), 1)
        first = jnp.sum(jnp.where(lane_row == 0, totals, 0.0), axis=1, keepdims=True)
        second = jnp.sum(jnp.where(lane_row == 1, totals, 0.0), axis=1, keepdims=True)
        return first, second

    def total_of(x):
        return jnp.sum(jnp.sum(x, axis=0, keepdims=True), axis=1, keepdims=True)

    quarter = pl.ds(pl.multiple_of(ray * 32, 32), 32)

    def field_copies(turn):
        src = full.at[turn].at[quarter]
        return [
            pltpu.make_async_remote_copy(
                src, src, near_send.at[turn, k - 1], near_recv.at[turn, k - 1],
                device_id=(vox, lax.rem(ray + k, n_ray)), device_id_type=MESH,
            )
            for k in range(1, n_ray)
        ]

    def halo_copies(turn):
        scaled = state.at[turn]
        right, left = lax.rem(vox + 1, n_vox), lax.rem(vox + n_vox - 1, n_vox)
        after, before = lax.rem(ray + 1, n_ray), lax.rem(ray + n_ray - 1, n_ray)
        plan = [
            (scaled, halo_x.at[turn, 0], (right, ray)),
            (scaled, halo_x.at[turn, 1], (left, ray)),
            (scaled.at[pl.ds(24, 8)], halo_y.at[turn, 0], (vox, after)),
            (scaled.at[pl.ds(0, 8)], halo_y.at[turn, 1], (vox, before)),
        ]
        return [
            pltpu.make_async_remote_copy(
                src, dst, near_send.at[turn, 3 + k], near_recv.at[turn, 3 + k],
                device_id=to, device_id_type=MESH,
            )
            for k, (src, dst, to) in enumerate(plan)
        ]

    def prior(turn):
        for copy in halo_copies(turn):
            copy.wait_recv()
        scaled = state[turn]
        place_of = iota(scaled.shape, 1)
        level = place_of // (columns * runs)
        column = lax.rem(place_of // runs, columns)
        row = iota(scaled.shape, 0)
        step = columns * runs
        zero = jnp.zeros_like(scaled)
        beside = jnp.where(level == 0, zero, pltpu.roll(scaled, step, 1))
        beside += jnp.where(level == levels - 1, zero, pltpu.roll(scaled, blocks - step, 1))
        edge = (columns - 1) * runs
        from_left = jnp.where(vox == 0, zero, pltpu.roll(halo_x[turn, 0], blocks - edge, 1))
        from_right = jnp.where(vox == n_vox - 1, zero, pltpu.roll(halo_x[turn, 1], edge, 1))
        beside += jnp.where(column == 0, from_left, pltpu.roll(scaled, runs, 1))
        beside += jnp.where(column == columns - 1, from_right, pltpu.roll(scaled, blocks - runs, 1))
        run = lax.rem(iota((1, blocks), 1), runs)
        last = halo_y[turn, 0][7:8]
        carried = jnp.where(run == 0, 0.0, pltpu.roll(halo_y[turn, 0], 1, 1)[7:8])
        low_row = jnp.where(ray == 0, carried, last)
        first = halo_y[turn, 1][0:1]
        carried = jnp.where(run == runs - 1, 0.0, pltpu.roll(halo_y[turn, 1], blocks - 1, 1)[0:1])
        high_row = jnp.where(ray == n_ray - 1, carried, first)
        beside += jnp.where(row == 0, low_row, pltpu.roll(scaled, 1, 0))
        beside += jnp.where(row == 31, high_row, pltpu.roll(scaled, 31, 0))
        return prior_t[quarter] * (6.0 * scaled - beside)

    ray_rows[:, :lanes] = dot(tile_hot[:, : observed_ref.shape[0]], observed_ref[...]).astype(BF16)
    transposed(1, 0, 1)
    tile_hot_t[...] = tile_hot[...].astype(F32).T.astype(BF16)
    prior_t[...] = prior_ref[...].T

    await_tiles(id_recv, 0, x_recv, 4)
    rows = n_dev * 4
    number = iota((1, blocks), 1).astype(F32)
    for q in range(4):

        def spread_ids(g, carry):
            at = pl.multiple_of(g * 64, 64)
            own = id_recv[pl.ds(at, 64)][:, q * 32 : q * 32 + 1]
            onehot[pl.ds(q * rows + at, 64)] = jnp.where(own == number, 1.0, 0.0).astype(BF16)
            return carry

        lax.fori_loop(0, rows // 64, spread_ids, 0)

    initial = place(1, 0)
    full[0, quarter] = initial
    gather(2, 0, initial)
    state[0] = prior_t[quarter] * initial
    for copy in halo_copies(0) + field_copies(0):
        copy.start()

    ray_high, ray_low = forward(2, 0)
    tiles = observed_ref.shape[0]
    rounded = ray_high[:tiles].astype(BF16)
    ray_rows[:, :lanes] = dot(tile_hot[:, :tiles], rounded).astype(BF16)
    transposed(3, 1, 1)
    prior_0 = prior(0)
    initial = full[0, quarter]
    curved = place(3, 1) + prior_0
    full[1, quarter] = curved
    gather(4, 1, curved)
    send_scalars(0, total_of(initial * initial), total_of(initial * curved))
    state[1] = prior_t[quarter] * curved
    for copy in halo_copies(1) + field_copies(1):
        copy.start()

    curved_high, curved_low = forward(4, 1)
    norm_0, bend_0 = await_scalars(0)
    step_0 = norm_0 / bend_0
    rays = (ray_high + ray_low) - step_0 * (curved_high + curved_low)
    both = jnp.concatenate(halves(rays[:tiles]), axis=1)
    ray_rows[...] = dot(tile_hot[:, :tiles], both).astype(BF16)
    transposed(5, 2, 2)
    residual = full[0, quarter] - step_0 * full[1, quarter]
    squares = total_of(residual * residual)
    send_scalars(1, squares, squares)
    known = prior_0 - step_0 * prior(1)
    norm_1, _ = await_scalars(1)
    ratio = norm_1 / norm_0
    direction = residual + ratio * full[0, quarter]
    curved = place(5, 2) + known + ratio * full[1, quarter]
    full[2, quarter] = curved
    for copy in field_copies(2):
        copy.start()
    bend = total_of(direction * curved)
    send_scalars(2, bend, bend)

    for turn in range(2):
        for copy in field_copies(turn):
            copy.wait_recv()
    start = full[0]
    residual = start - step_0 * full[1]
    direction = residual + ratio * start
    before = (step_0 * start).T
    residual_t = residual.T
    direction_t = direction.T
    for copy in field_copies(2):
        copy.wait_recv()
    curved_t = full[2].T
    bend_1, _ = await_scalars(2)
    step_1 = norm_1 / bend_1
    solution_ref[...] = before + step_1 * direction_t
    residual_ref[...] = residual_t - step_1 * curved_t

    await_tiles(id_recv, 0, x_send, 4)
    for phase, buffer in ((1, 0), (3, 1), (5, 2)):
        await_tiles(prod_recv.at[buffer], phase, x_send, 4)
    for phase, buffer in ((2, 0), (4, 1)):
        await_tiles(pick_recv.at[buffer], phase, x_send, 4)
    for turn in range(3):
        await_tiles(scalar_recv.at[turn], 6 + turn, x_send, 1)
        for copy in field_copies(turn):
            copy.wait_send()
    for turn in range(2):
        for copy in halo_copies(turn):
            copy.wait_send()


def on_device(weights, slot_block, slot_tile, slot_count, observed, prior_scale):
    n_vox, n_ray = lax.axis_size("vox"), lax.axis_size("ray")
    n_dev = n_vox * n_ray
    levels, columns, across = prior_scale.shape
    slots, lanes = weights.shape[2], weights.shape[4]
    runs = across // lanes
    blocks = levels * columns * runs
    vmem = pl.BlockSpec(memory_space=pltpu.VMEM)
    outs = pl.pallas_call(
        functools.partial(kernel, n_vox, n_ray, (levels, columns, runs, lanes)),
        out_shape=[jax.ShapeDtypeStruct((blocks, lanes), F32)] * 2,
        in_specs=[pl.BlockSpec(memory_space=pl.ANY)] + [vmem] * 5,
        out_specs=[vmem, vmem],
        scratch_shapes=[
            pltpu.VMEM((n_vox, slots, lanes, lanes), BF16),
            pltpu.VMEM((n_dev * slots, blocks), BF16),
            pltpu.VMEM((n_vox * slots, lanes), BF16),
            pltpu.VMEM((lanes, n_vox * slots), BF16),
            pltpu.VMEM((n_vox * slots, 2 * lanes), BF16),
            pltpu.VMEM((2, n_vox * slots, lanes), F32),
            pltpu.VMEM((lanes, blocks), F32),
            pltpu.VMEM((n_vox * 4, lanes), F32),
            pltpu.VMEM((n_dev * 4, lanes), F32),
            pltpu.VMEM((3, n_dev * 4, lanes), F32),
            pltpu.VMEM((3, n_dev * 4, lanes), F32),
            pltpu.VMEM((2, n_dev * 4, lanes), F32),
            pltpu.VMEM((2, n_dev * 4, lanes), F32),
            pltpu.VMEM((3, 8, lanes), F32),
            pltpu.VMEM((3, n_dev, lanes), F32),
            pltpu.VMEM((2, 32, blocks), F32),
            pltpu.VMEM((2, 2, 32, blocks), F32),
            pltpu.VMEM((2, 2, 8, blocks), F32),
            pltpu.VMEM((3, lanes, blocks), F32),
            pltpu.SemaphoreType.DMA((n_vox // 2,)),
            pltpu.SemaphoreType.DMA((9,)),
            pltpu.SemaphoreType.DMA((9,)),
            pltpu.SemaphoreType.DMA((3, 7)),
            pltpu.SemaphoreType.DMA((3, 7)),
            pltpu.SemaphoreType.DMA,
        ],
        compiler_params=pltpu.CompilerParams(
            collective_id=0, has_side_effects=True, vmem_limit_bytes=52 * 2**20
        ),
        name="tomography",
    )(
        weights[:, 0],
        slot_block[:, 0].T,
        slot_tile[:, 0].T,
        slot_count.T,
        observed[:, 0],
        prior_scale.reshape(blocks, lanes),
    )
    return tuple(out.reshape(levels, columns, across) for out in outs)


def solution(mesh):
    in_specs = (
        P("vox", "ray", None, None, None),
        P("vox", "ray", None),
        P("vox", "ray", None),
        P("vox", "ray"),
        P("vox", "ray", None),
        P(None, "vox", None),
    )
    out_specs = (P(None, "vox", None), P(None, "vox", None))
    return jax.shard_map(
        on_device, mesh=mesh, in_specs=in_specs, out_specs=out_specs, check_vma=False
    )
```

time: 496 us -> 106 us (0.21)
  blocking collectives: 197 us -> 0 us
  waiting for transfers between devices: 139 us -> 0 us
  Pallas kernels: 0 us -> 98.7 us
  starting transfers between devices: 50.2 us -> 0 us
  matrix products: 49.6 us -> 0 us
  other arithmetic: 27.1 us -> 0 us
  between operations: 18.2 us -> 0.65 us
  local copies, waits for them, and re-layouts: 12.1 us -> 5.94 us
    psum x3 -> x0, blocking collectives: 197 us -> none  [the longest x2 131 us: squares_here(): return lax.psum(jnp.sum(vector * vector), 'vox')]
    psum x3 -> x0, waiting for transfers between devices: 111 us -> none  [combine(): grouped = lax.psum(place(used_part, wanted_flat), 'ray')]
    pallas_call x0 -> x1, Pallas kernels: none -> 98.7 us  [on_device(): pl.pallas_call(functools.partial(kernel, n_vox, n_ray, (levels, columns,...]
    dot_general x7 -> x0, matrix products: 49.6 us -> none  [the longest x2 24.5 us: forward(): jnp.einsum('ustb,usb->ust', tile_weights, fetched, preferred_element_type...]
    all_to_all x6 -> x0, starting transfers between devices: 38.7 us -> none  [the longest x3 15.2 us: transposed(): lax.all_to_all(voxel_part, 'vox', split_axis=0, concat_axis=0, tiled=True)]
    all_to_all x6 -> x0, waiting for transfers between devices: 28.3 us -> none  [the longest x2 14.6 us: forward(): lax.all_to_all(picked, 'vox', split_axis=0, concat_axis=0, tiled=True)]
    ppermute x4 -> x0, starting transfers between devices: 11.3 us -> none  [the longest x2 7.09 us: padded_2(): lax.ppermute(lax.slice_in_dim(block, block.shape[dim] - width, None, axis...]
    scatter-add x3 -> x0, other arithmetic: 9.06 us -> none  [place(): jnp.zeros((block_total, block_len), jnp.float32).at[targets].add(rows)]
  transfers between devices with their start and end apart: 13 -> 0, of which waited for: 8 -> 0; matrix products, arithmetic and copies ran while one was open for 5% -> 0% of each run, Pallas kernels for 0% -> 0%
where the time goes in v1:
time: 106 us; the launch traced here: 105 us
  Pallas kernels  98.7 us (93%)
  local copies, waits for them, and re-layouts  5.94 us (6%)
    pallas_call x1, Pallas kernels, on_device(): pl.pallas_call(functools.partial(kernel, n_vox, n_ray, (levels, columns,...  98.7 us
    unnamed x8, local copies, waits for them, and re-layouts  2.76 us

profile of v1, /device:TPU:1, one launch (start us, length us, event | category | flops | bytes accessed | tf_op | source)
XLA Modules:
  0.0 105.3 jit_solution(3525175382714564360)
XLA Ops:
  0.6 1.3 %reshape.13.prior_ref = f32[1024,128]{1,0:T(8,128)S(1)} reshape(f32[32,4,1024]{2,1,0:T(4,128)} %param.11) | data formatting | bytes 1048576 | tf_op jit(solution)/shard_map/reshape | solution.py:477
  1.9 0.0 copy-start
  1.9 0.7 copy-done
  2.6 0.0 copy-start.1
  2.6 0.7 copy-done.1
  3.3 0.0 copy-start.2
  3.3 0.7 copy-done.2
  4.0 0.0 copy-start.3
  4.0 0.7 copy-done.3
  4.7 98.7 %tomography.1 = (f32[1024,128]{1,0:T(8,128)S(1)}, f32[1024,128]{1,0:T(8,128)S(1)}) custom-call(bf16[32,16,128,128]{3,2,1,0:T(8,128)(2,1)} %bitcast.13, s32[16,32]{1,0:T(8,128)S(1)} %bitcast.10, s32[16,32]{1,0:T(8,128)S(1)} %bitcast.11, s32[1,32]{1,0:T(1,128)S(1)} %bitcast.12, bf16[64,128]{1,0:T(8,128)(2,1)S(1)} %bitcast.9, f32[1024,128]{1,0:T(8,128)S(1)} %reshape.13.prior_ref), custom_call_target="tpu_custom_call" | custom-call | tf_op jit(solution)/shard_map/tomography/pallas_call | solution.py:435
  103.4 1.0 reshape.14
  104.4 1.0 reshape.15
Async XLA Ops:
  1.9 0.7 copy-start
  2.6 0.7 copy-start.1
  3.3 0.7 copy-start.2
  4.0 0.7 copy-start.3

commit v2 on v1

v2 whole, which is shorter than its diff:
```python
import functools

import jax
import jax.numpy as jnp
from jax import lax
from jax.experimental import pallas as pl
from jax.experimental.pallas import tpu as pltpu
from jax.sharding import PartitionSpec as P

F32 = jnp.float32
BF16 = jnp.bfloat16
MESH = pl.DeviceIdType.MESH
NT = (((1,), (1,)), ((), ()))


def dot(a, b):
    return jnp.dot(a, b, preferred_element_type=F32)


def dot_nt(a, b):
    return lax.dot_general(a, b, NT, preferred_element_type=F32)


def iota(shape, dim):
    return lax.broadcasted_iota(jnp.int32, shape, dim)


def halves(x):
    high = x.astype(BF16)
    return high, (x - high.astype(F32)).astype(BF16)


def block_transpose(a):
    which = lax.rem(iota(a.shape, 1) // 32 - iota(a.shape, 0) // 4 + 4, 4)
    out = a
    for step in range(1, 4):
        moved = pltpu.roll(pltpu.roll(a, 32 * step, 1), 16 - 4 * step, 0)
        out = jnp.where(which == step, moved, out)
    return out


def block_diagonal(rows):
    slots, length = rows.shape
    wide = jnp.concatenate([rows] * slots, axis=1)
    own = iota(wide.shape, 0) == iota(wide.shape, 1) // length
    return jnp.where(own, wide, jnp.zeros_like(wide))


def kernel(
    n_vox, n_ray, dims,
    w_hbm, block_hbm, tile_hbm, count_hbm, observed_hbm, prior_hbm,
    solution_ref, residual_ref,
    block_ref, tile_ref, count_ref, observed_ref, prior_ref,
    w, onehot, id_wide, tile_hot, tile_hot_t, ray_rows, ray_part, prior_t,
    id_send, id_recv, prod_send, prod_recv, pick_send, pick_recv,
    scalar_ray, scalar_vox, prior_keep, curved_keep, ray_keep, state, face, halo_x, halo_y, own, shared,
    in_sem, w_sem, pick_sem, x_send, x_recv, near_send, near_recv, local_sem,
):
    levels, columns, runs, lanes = dims
    n_dev = n_vox * n_ray
    pairs = n_vox // 2
    blocks = levels * columns * runs
    vox = lax.axis_index("vox")
    ray = lax.axis_index("ray")
    me = vox * n_ray + ray

    small = [
        pltpu.make_async_copy(src, dst, in_sem.at[k])
        for k, (src, dst) in enumerate((
            (tile_hbm, tile_ref), (count_hbm, count_ref), (block_hbm, block_ref),
            (observed_hbm, observed_ref), (prior_hbm, prior_ref),
        ))
    ]
    for copy in small:
        copy.start()

    side_y = 4
    side_z = pairs // side_y
    my_z, my_y = vox // 2 // side_y, lax.rem(vox // 2, side_y)

    def ring(k):
        return k + (k // 2) * (1 - 2 * lax.rem(k, 2))

    def near_pair(p):
        z = lax.rem(my_z + ring(p // side_y), side_z)
        return z * side_y + lax.rem(my_y + ring(lax.rem(p, side_y)), side_y)

    def far_pair(p):
        return near_pair(pairs - 1 - p)

    def w_copy(p):
        at = pl.ds(2 * far_pair(p), 2)
        return pltpu.make_async_copy(w_hbm.at[at], w.at[at], w_sem.at[p])

    barrier = pltpu.get_barrier_semaphore()
    core = lax.rem(vox, 2)
    rays = [lax.rem(ray + k, n_ray) for k in range(n_ray)]

    def peers(pair):
        return [(2 * pair + c, r) for c in range(2) for r in rays]

    def own_peers():
        return [(vox + 1 - 2 * core, r) for r in rays] + [(vox, r) for r in rays[1:]]

    def for_all(act, group=3):
        def step(g, carry):
            for j in range(group):
                for to in peers(far_pair(group * g + j)):
                    act(to)
            return carry

        lax.fori_loop(0, (pairs - 1) // group, step, 0)
        for to in own_peers():
            act(to)

    def for_vox(act, group=3):
        def step(g, carry):
            for j in range(group):
                pair = far_pair(group * g + j)
                act((2 * pair, ray))
                act((2 * pair + 1, ray))
            return carry

        lax.fori_loop(0, (pairs - 1) // group, step, 0)
        act((vox + 1 - 2 * core, ray))

    def greet(to):
        pl.semaphore_signal(barrier, 1, device_id=to, device_id_type=MESH)

    def start_w(p, carry):
        w_copy(p).start()
        return carry

    lax.fori_loop(0, pairs, start_w, 0)
    for_all(greet)

    def rows4(index):
        return pl.ds(pl.multiple_of(index * 4, 4), 4)

    def send_tile(src, dst, phase, to):
        pltpu.make_async_remote_copy(
            src, dst.at[rows4(me)], x_send.at[phase], x_recv.at[phase],
            device_id=to, device_id_type=MESH,
        ).start()

    def keep_tile(src, dst, phase):
        return pltpu.make_async_copy(src, dst.at[rows4(me)], local_sem.at[phase])

    def await_tiles(dst, phase, sems, rows):
        part = dst.at[pl.ds(0, (n_dev - 1) * rows)]
        pltpu.make_async_copy(part, part, sems.at[phase]).wait()

    for copy in small:
        copy.wait()
    slots = tile_ref.shape[0]
    live = iota((slots, n_vox), 0) < count_ref[...]
    tiles_live = jnp.where(live, tile_ref[...], -1)
    ids = jnp.concatenate(
        [block_ref[...].astype(F32), jnp.zeros((lanes - slots, n_vox), F32)], axis=0
    )
    id_send[...] = ids.T.reshape(n_vox, 1, lanes)
    lane = iota((slots, lanes), 1)
    for u in range(n_vox):
        at = pl.ds(u * slots, slots)
        hot = jnp.where(tiles_live[:, u : u + 1] == lane, 1.0, 0.0)
        tile_hot[at] = hot.astype(BF16)

    def send_id(to):
        pltpu.make_async_remote_copy(
            id_send.at[to[0]], id_recv.at[me], x_send.at[0], x_recv.at[0],
            device_id=to, device_id_type=MESH,
        ).start()

    def await_ids(sems):
        part = id_recv.at[pl.ds(0, n_dev - 1)]
        pltpu.make_async_copy(part, part, sems.at[0]).wait()

    def transposed(phase, buffer, parts, midway=None):
        def send(to):
            src = prod_send.at[buffer].at[rows4(to[0] * n_ray + to[1])]
            send_tile(src, prod_recv.at[buffer], phase, to)

        def product(pair):
            left = []
            for u in (2 * pair, 2 * pair + 1):
                rows = ray_rows[pl.ds(pl.multiple_of(u * slots, slots), slots)]
                for part in range(parts):
                    left.append(block_diagonal(rows[:, part * lanes : (part + 1) * lanes]))
            right = jnp.concatenate(
                [w[2 * pair].reshape(-1, lanes), w[2 * pair + 1].reshape(-1, lanes)], axis=1
            )
            made = dot(jnp.concatenate(left, axis=0), right)
            out = []
            for side in range(2):
                columns_of = slice(side * lanes, (side + 1) * lanes)
                base = side * parts * slots
                rows = made[base : base + slots, columns_of]
                for part in range(1, parts):
                    rows = rows + made[base + part * slots : base + (part + 1) * slots, columns_of]
                out.append(block_transpose(rows))
            return jnp.concatenate(out, axis=0)

        def work(places):
            chosen = [far_pair(p) for p in places]
            if phase == 1:
                for p in places:
                    w_copy(p).wait()
            made = [product(pair) for pair in chosen]
            for pair, tile in zip(chosen, made):
                at = pl.ds(pl.multiple_of(pair * 2 * slots, 2 * slots), 2 * slots)
                prod_send[buffer, at] = tile
            return chosen

        group = 3

        def step(g, carry):
            chosen = work([group * g + j for j in range(group)])
            if phase > 1:
                for pair in chosen:
                    for to in peers(pair):
                        send(to)
            return carry

        groups = (pairs - 1) // group
        cut = groups if midway is None else groups * 3 // 5
        lax.fori_loop(0, cut, step, 0)
        if midway is not None:
            midway()
            lax.fori_loop(cut, groups, step, 0)
        work([pairs - 1])
        keep_tile(prod_send.at[buffer].at[rows4(me)], prod_recv.at[buffer], phase).start()
        if phase == 1:
            pl.semaphore_wait(barrier, n_dev - 1)
            for_all(send_id)
            for_all(send)
            id_recv[me] = id_send[vox]
        else:
            for to in own_peers():
                send(to)

    def place(phase, buffer):
        keep_tile(prod_send.at[buffer].at[rows4(me)], prod_recv.at[buffer], phase).wait()
        await_tiles(prod_recv.at[buffer], phase, x_recv, 4)
        turned = prod_recv[buffer].T
        rows = turned.shape[1]
        total = None
        for q in range(4):
            high, low = halves(turned[q * 32 : (q + 1) * 32])
            part = dot(
                jnp.concatenate([high, low], axis=0), onehot[q * rows : (q + 1) * rows]
            )
            total = part if total is None else total + part
        return total[:32] + total[32:]

    def gather(phase, buffer, values):
        high, low = halves(values)
        both = jnp.concatenate([high, low], axis=0)
        rows = n_dev * 4
        chunk = rows // side_z

        def send(to):
            pltpu.make_async_remote_copy(
                pick_send.at[buffer].at[rows4(to[0] * n_ray + to[1])],
                pick_recv.at[buffer].at[rows4(me)],
                x_send.at[phase], pick_sem.at[buffer, vox // 2],
                device_id=to, device_id_type=MESH,
            ).start()

        for near in (0, 1, 3, 2):
            z = lax.rem(my_z + near, side_z)
            picked = [
                onehot[pl.ds(pl.multiple_of(q * rows + z * chunk, chunk), chunk)] for q in range(4)
            ]
            got = dot_nt(both, jnp.concatenate(picked, axis=0))
            got = got[:32] + got[32:]
            pieces = [got[:, q * chunk : (q + 1) * chunk] for q in range(4)]
            pick_send[buffer, pl.ds(pl.multiple_of(z * chunk, chunk), chunk)] = jnp.concatenate(
                pieces, axis=0
            ).T
            for beside in (0, 1, 3, 2):
                pair = z * side_y + lax.rem(my_y + beside, side_y)
                for to in own_peers() if near == beside == 0 else peers(pair):
                    send(to)
        keep_tile(pick_send.at[buffer].at[rows4(me)], pick_recv.at[buffer], phase).start()

    def forward(phase, buffer, midway):
        def work(places, tiles):
            chosen = [near_pair(p) for p in places]
            for pair in chosen:
                at = pl.ds(pl.multiple_of(pair * 2 * slots, 2 * slots), tiles * 4)
                part = pick_recv.at[buffer].at[at]
                pltpu.make_async_copy(part, part, pick_sem.at[buffer, pair]).wait()
            results = []
            for pair in chosen:
                left = []
                for side in range(2):
                    at = pl.ds(pl.multiple_of((2 * pair + side) * slots, slots), slots)
                    high, low = halves(block_transpose(pick_recv[buffer, at]))
                    left += [block_diagonal(high), block_diagonal(low)]
                right = jnp.concatenate(
                    [
                        jnp.concatenate([w[2 * pair + side, s] for s in range(slots)], axis=1)
                        for side in range(2)
                    ],
                    axis=0,
                )
                results.append(dot_nt(jnp.concatenate(left, axis=0), right))
            for pair, made in zip(chosen, results):
                for side in range(2):
                    at = pl.ds(pl.multiple_of((2 * pair + side) * slots, slots), slots)
                    columns_of = slice(side * lanes, (side + 1) * lanes)
                    for part in range(2):
                        base = (2 * side + part) * slots
                        ray_part[part, at] = made[base : base + slots, columns_of]

        group = 3

        def step(g, carry):
            work([group * g + j + 1 for j in range(group)], 2 * n_ray)
            return carry

        keep_tile(pick_send.at[buffer].at[rows4(me)], pick_recv.at[buffer], phase).wait()
        work([0], 2 * n_ray - 1)
        groups = (pairs - 1) // group
        cut = groups * 2 // 5
        lax.fori_loop(0, cut, step, 0)
        midway()
        lax.fori_loop(cut, groups, step, 0)

        def tiles_of(part):
            values = ray_part[part]
            a, rest = halves(values)
            rest = values - a.astype(F32)
            b = rest.astype(BF16)
            c = (rest - b.astype(F32)).astype(BF16)
            return dot(tile_hot_t[...], a) + dot(tile_hot_t[...], b) + dot(tile_hot_t[...], c)

        return tiles_of(0), tiles_of(1)

    lane_row = iota((1, lanes), 1)

    def sum_along_ray(turn, parts):
        row = jnp.zeros((1, lanes), F32)
        for k, part in enumerate(parts):
            row = jnp.where(lane_row == k, part, row)
        scalar_ray[turn, ray] = row
        src = scalar_ray.at[turn, ray]
        for k in range(1, n_ray):
            pltpu.make_async_remote_copy(
                src, src, x_send.at[6 + turn], x_recv.at[6 + turn],
                device_id=(vox, rays[k]), device_id_type=MESH,
            ).start()

    def await_rows(buffer, sems, at, count):
        part = buffer.at[pl.ds(0, count)]
        pltpu.make_async_copy(part, part, sems.at[at]).wait()

    def sum_along_vox(turn):
        await_rows(scalar_ray.at[turn], x_recv, 6 + turn, n_ray - 1)
        scalar_vox[turn, vox] = jnp.sum(scalar_ray[turn], axis=0)
        src = scalar_vox.at[turn, vox]

        def send(to):
            pltpu.make_async_remote_copy(
                src, src, x_send.at[8 + turn], x_recv.at[8 + turn],
                device_id=to, device_id_type=MESH,
            ).start()

        for_vox(send)

    def totals(turn, count):
        await_rows(scalar_vox.at[turn], x_recv, 8 + turn, n_vox - 1)
        row = jnp.sum(scalar_vox[turn], axis=0)
        return [
            jnp.sum(jnp.where(lane_row == k, row, 0.0), axis=1, keepdims=True)
            for k in range(count)
        ]

    def total_of(x):
        return jnp.sum(jnp.sum(x, axis=0, keepdims=True), axis=1, keepdims=True)

    quarter = pl.ds(pl.multiple_of(ray * 32, 32), 32)

    def field_copies(turn):
        src = shared.at[turn].at[quarter]
        return [
            pltpu.make_async_remote_copy(
                src, src, near_send.at[turn, k - 1], near_recv.at[turn, k - 1],
                device_id=(vox, lax.rem(ray + k, n_ray)), device_id_type=MESH,
            )
            for k in range(1, n_ray)
        ]

    def halo_copies(turn):
        scaled = state.at[turn]
        right, left = lax.rem(vox + 1, n_vox), lax.rem(vox + n_vox - 1, n_vox)
        after, before = lax.rem(ray + 1, n_ray), lax.rem(ray + n_ray - 1, n_ray)
        plan = [
            (face.at[turn, 0], halo_x.at[turn, 0], (right, ray)),
            (face.at[turn, 1], halo_x.at[turn, 1], (left, ray)),
            (scaled.at[pl.ds(24, 8)], halo_y.at[turn, 0], (vox, after)),
            (scaled.at[pl.ds(0, 8)], halo_y.at[turn, 1], (vox, before)),
        ]
        return [
            pltpu.make_async_remote_copy(
                src, dst, near_send.at[turn, 3 + k], near_recv.at[turn, 3 + k],
                device_id=to, device_id_type=MESH,
            )
            for k, (src, dst, to) in enumerate(plan)
        ]

    def column_at(size):
        return lax.rem(iota((32, size), 1) // runs, columns)

    def start_prior(turn, field):
        scaled = prior_t[quarter] * field
        state[turn] = scaled
        for side, column in ((0, columns - 1), (1, 0)):
            for k in range(blocks // lanes // columns):
                packed = jnp.zeros((32, lanes), F32)
                for m in range(columns):
                    at = (columns * k + m) * lanes
                    moved = scaled[:, at : at + lanes]
                    shift = (runs * (m - column)) % lanes
                    if shift:
                        moved = pltpu.roll(moved, shift, 1)
                    packed = jnp.where(column_at(lanes) == m, moved, packed)
                face[turn, side, :, k * lanes : (k + 1) * lanes] = packed
        for copy in halo_copies(turn):
            copy.start()

    def unpacked(turn, side, column):
        out = []
        for k in range(blocks // lanes // columns):
            packed = halo_x[turn, side, :, k * lanes : (k + 1) * lanes]
            for m in range(columns):
                shift = (runs * (column - m)) % lanes
                out.append(pltpu.roll(packed, shift, 1) if shift else packed)
        return jnp.concatenate(out, axis=1)

    def prior(turn):
        for copy in halo_copies(turn):
            copy.wait_recv()
        scaled = state[turn]
        place_of = iota(scaled.shape, 1)
        level = place_of // (columns * runs)
        column = lax.rem(place_of // runs, columns)
        row = iota(scaled.shape, 0)
        step = columns * runs
        zero = jnp.zeros_like(scaled)
        beside = jnp.where(level == 0, zero, pltpu.roll(scaled, step, 1))
        beside += jnp.where(level == levels - 1, zero, pltpu.roll(scaled, blocks - step, 1))
        from_left = jnp.where(vox == 0, zero, unpacked(turn, 0, 0))
        from_right = jnp.where(vox == n_vox - 1, zero, unpacked(turn, 1, columns - 1))
        beside += jnp.where(column == 0, from_left, pltpu.roll(scaled, runs, 1))
        beside += jnp.where(column == columns - 1, from_right, pltpu.roll(scaled, blocks - runs, 1))
        run = lax.rem(iota((1, blocks), 1), runs)
        last = halo_y[turn, 0][7:8]
        carried = jnp.where(run == 0, 0.0, pltpu.roll(halo_y[turn, 0], 1, 1)[7:8])
        low_row = jnp.where(ray == 0, carried, last)
        first = halo_y[turn, 1][0:1]
        carried = jnp.where(run == runs - 1, 0.0, pltpu.roll(halo_y[turn, 1], blocks - 1, 1)[0:1])
        high_row = jnp.where(ray == n_ray - 1, carried, first)
        beside += jnp.where(row == 0, low_row, pltpu.roll(scaled, 1, 0))
        beside += jnp.where(row == 31, high_row, pltpu.roll(scaled, 31, 0))
        return prior_t[quarter] * (6.0 * scaled - beside)

    ray_rows[:, :lanes] = dot(tile_hot[:, : observed_ref.shape[0]], observed_ref[...]).astype(BF16)
    transposed(1, 0, 1)
    tile_hot_t[...] = tile_hot[...].astype(F32).T.astype(BF16)
    prior_t[...] = prior_ref[...].reshape(blocks, lanes).T

    await_ids(x_recv)
    rows = n_dev * 4
    number = iota((1, blocks), 1).astype(F32)
    low_slot, low_lane = lax.rem(iota((rows, lanes), 0), 4), iota((rows, lanes), 1)
    fourfold = jnp.where(iota((rows, n_dev), 0) // 4 == iota((rows, n_dev), 1), 1.0, 0.0)
    fourfold = fourfold.astype(BF16)
    id_high, id_low = halves(id_recv[...].reshape(n_dev, lanes))
    repeated = dot(fourfold, id_high) + dot(fourfold, id_low)
    ones = jnp.full((lanes, lanes), 1.0, BF16)
    for q in range(4):
        high, low = halves(jnp.where(low_lane == 4 * q + low_slot, repeated, 0.0))
        id_wide[q] = dot(high, ones) + dot(low, ones)

    def spread_ids(g, carry):
        at = pl.multiple_of(g * 32, 32)
        for q in range(4):
            own = jnp.concatenate([id_wide[q, pl.ds(at, 32)]] * (blocks // lanes), axis=1)
            onehot[pl.ds(q * rows + at, 32)] = jnp.where(own == number, 1.0, 0.0).astype(BF16)
        return carry

    lax.fori_loop(0, rows // 32, spread_ids, 0)

    initial = place(1, 0)
    own[0] = initial
    gather(2, 0, initial)
    start_prior(0, initial)
    shared[0, quarter] = initial.astype(BF16)

    def prior_0():
        for copy in field_copies(0):
            copy.start()
        prior_keep[0] = prior(0)

    tiles = observed_ref.shape[0]
    ray_high, ray_low = forward(2, 0, prior_0)
    rounded = ray_high[:tiles].astype(BF16)
    rays_0 = ray_high[:tiles] + ray_low[:tiles]
    ray_keep[0] = rays_0
    ray_keep[1] = rounded.astype(F32)
    ray_rows[:, :lanes] = dot(tile_hot[:, :tiles], rounded).astype(BF16)
    initial = own[0]
    bend = total_of(rays_0 * rounded.astype(F32)) + total_of(initial * prior_keep[0])
    sum_along_ray(0, [total_of(initial * initial), bend])
    transposed(3, 1, 1, lambda: sum_along_vox(0))
    norm_0, bend_0 = totals(0, 2)
    step_0 = norm_0 / bend_0
    curved = place(3, 1) + prior_keep[0]
    curved_keep[...] = curved
    residual = own[0] - step_0 * curved
    own[1] = residual
    gather(4, 1, residual)
    start_prior(1, residual)
    shared[1, quarter] = residual.astype(BF16)

    def prior_1():
        for copy in field_copies(1):
            copy.start()
        prior_keep[1] = prior(1)

    ray_high, ray_low = forward(4, 1, prior_1)
    rays_1 = ray_high[:tiles] + ray_low[:tiles]
    both = jnp.concatenate(halves(rays_1), axis=1)
    ray_rows[...] = dot(tile_hot[:, :tiles], both).astype(BF16)
    initial, residual = own[0], own[1]
    square = total_of(rays_1 * rays_1) + total_of(residual * prior_keep[1])
    cross = total_of(rays_1 * (ray_keep[0] + ray_keep[1]))
    cross += total_of(initial * prior_keep[1] + residual * prior_keep[0])
    sum_along_ray(1, [total_of(residual * residual), square, cross])
    transposed(5, 2, 2, lambda: sum_along_vox(1))
    norm_1, square, cross = totals(1, 3)
    ratio = norm_1 / norm_0
    step_1 = norm_1 / (square + ratio * (cross + ratio * bend_0))

    for turn in range(2):
        for copy in field_copies(turn):
            copy.wait_recv()
    start, later = shared[0].astype(F32), shared[1].astype(F32)
    solution_ref[...] = (step_0 * start + step_1 * (later + ratio * start)).T
    curved = place(5, 2) + prior_keep[1] + ratio * curved_keep[...]
    shared[2, quarter] = (own[1] - step_1 * curved).astype(BF16)
    for copy in field_copies(2):
        copy.start()
    for copy in field_copies(2):
        copy.wait_recv()
    residual_ref[...] = shared[2].astype(F32).T

    await_ids(x_send)
    for phase, buffer in ((1, 0), (3, 1), (5, 2)):
        await_tiles(prod_recv.at[buffer], phase, x_send, 4)
    for phase, buffer in ((2, 0), (4, 1)):
        await_tiles(pick_recv.at[buffer], phase, x_send, 4)
    for turn in range(2):
        await_rows(scalar_ray.at[turn], x_send, 6 + turn, n_ray - 1)
        await_rows(scalar_vox.at[turn], x_send, 8 + turn, n_vox - 1)
    for turn in range(3):
        for copy in field_copies(turn):
            copy.wait_send()
    for turn in range(2):
        for copy in halo_copies(turn):
            copy.wait_send()


def on_device(weights, slot_block, slot_tile, slot_count, observed, prior_scale):
    n_vox, n_ray = lax.axis_size("vox"), lax.axis_size("ray")
    n_dev = n_vox * n_ray
    levels, columns, across = prior_scale.shape
    slots, lanes = weights.shape[2], weights.shape[4]
    runs = across // lanes
    blocks = levels * columns * runs
    vmem = pl.BlockSpec(memory_space=pltpu.VMEM)
    outs = pl.pallas_call(
        functools.partial(kernel, n_vox, n_ray, (levels, columns, runs, lanes)),
        out_shape=[jax.ShapeDtypeStruct((blocks, lanes), F32)] * 2,
        in_specs=[pl.BlockSpec(memory_space=pltpu.HBM)] * 6,
        out_specs=[vmem, vmem],
        scratch_shapes=[
            pltpu.VMEM((slots, n_vox), jnp.int32),
            pltpu.VMEM((slots, n_vox), jnp.int32),
            pltpu.VMEM((1, n_vox), jnp.int32),
            pltpu.VMEM(observed[:, 0].shape, BF16),
            pltpu.VMEM(prior_scale.shape, F32),
            pltpu.VMEM((n_vox, slots, lanes, lanes), BF16),
            pltpu.VMEM((n_dev * slots, blocks), BF16),
            pltpu.VMEM((4, n_dev * 4, lanes), F32),
            pltpu.VMEM((n_vox * slots, lanes), BF16),
            pltpu.VMEM((lanes, n_vox * slots), BF16),
            pltpu.VMEM((n_vox * slots, 2 * lanes), BF16),
            pltpu.VMEM((2, n_vox * slots, lanes), F32),
            pltpu.VMEM((lanes, blocks), F32),
            pltpu.VMEM((n_vox, 1, lanes), F32),
            pltpu.VMEM((n_dev, 1, lanes), F32),
            pltpu.VMEM((3, n_dev * 4, lanes), F32),
            pltpu.VMEM((3, n_dev * 4, lanes), F32),
            pltpu.VMEM((2, n_dev * 4, lanes), F32),
            pltpu.VMEM((2, n_dev * 4, lanes), F32),
            pltpu.VMEM((2, n_ray, 1, lanes), F32),
            pltpu.VMEM((2, n_vox, 1, lanes), F32),
            pltpu.VMEM((2, 32, blocks), F32),
            pltpu.VMEM((32, blocks), F32),
            pltpu.VMEM((2, observed.shape[0], lanes), F32),
            pltpu.VMEM((2, 32, blocks), F32),
            pltpu.VMEM((2, 2, 32, blocks // columns), F32),
            pltpu.VMEM((2, 2, 32, blocks // columns), F32),
            pltpu.VMEM((2, 2, 8, blocks), F32),
            pltpu.VMEM((2, 32, blocks), F32),
            pltpu.VMEM((3, lanes, blocks), BF16),
            pltpu.SemaphoreType.DMA((5,)),
            pltpu.SemaphoreType.DMA((n_vox // 2,)),
            pltpu.SemaphoreType.DMA((2, n_vox // 2)),
            pltpu.SemaphoreType.DMA((10,)),
            pltpu.SemaphoreType.DMA((10,)),
            pltpu.SemaphoreType.DMA((3, 7)),
            pltpu.SemaphoreType.DMA((3, 7)),
            pltpu.SemaphoreType.DMA((6,)),
        ],
        compiler_params=pltpu.CompilerParams(
            collective_id=0, has_side_effects=True, vmem_limit_bytes=64 * 2**20
        ),
        name="tomography",
    )(
        weights[:, 0],
        slot_block[:, 0].T,
        slot_tile[:, 0].T,
        slot_count.T,
        observed[:, 0],
        prior_scale,
    )
    return tuple(out.reshape(levels, columns, across) for out in outs)


def solution(mesh):
    in_specs = (
        P("vox", "ray", None, None, None),
        P("vox", "ray", None),
        P("vox", "ray", None),
        P("vox", "ray"),
        P("vox", "ray", None),
        P(None, "vox", None),
    )
    out_specs = (P(None, "vox", None), P(None, "vox", None))
    return jax.shard_map(
        on_device, mesh=mesh, in_specs=in_specs, out_specs=out_specs, check_vma=False
    )
```

time: 106 us -> 83.1 us (0.78)
  Pallas kernels: 98.7 us -> 78.3 us
  local copies, waits for them, and re-layouts: 5.94 us -> 4.01 us
    pallas_call x1, Pallas kernels: 98.7 us -> 78.3 us  [on_device(): pl.pallas_call(functools.partial(kernel, n_vox, n_ray, (levels, columns,...]
    unnamed x8 -> x0, local copies, waits for them, and re-layouts: 2.76 us -> none
    reshape x2, local copies, waits for them, and re-layouts: 1.93 us -> 4.01 us  [on_device(): return tuple((out.reshape(levels, columns, across) for out in outs))]
    reshape x1 -> x0, local copies, waits for them, and re-layouts: 1.25 us -> none  [on_device(): prior_scale.reshape(blocks, lanes)]
where the time goes in v2:
time: 83.1 us; the launch traced here: 82.9 us
  Pallas kernels  78.3 us (94%)
  local copies, waits for them, and re-layouts  4.01 us (5%)
    pallas_call x1, Pallas kernels, on_device(): pl.pallas_call(functools.partial(kernel, n_vox, n_ray, (levels, columns,...  78.3 us
    reshape x2, local copies, waits for them, and re-layouts, on_device(): return tuple((out.reshape(levels, columns, across) for out in outs))  4.01 us

profile of v2, /device:TPU:1, one launch (start us, length us, event | category | flops | bytes accessed | tf_op | source)
XLA Modules:
  0.0 82.9 jit_solution(17220623801552879325)
XLA Ops:
  0.6 78.3 %tomography.1 = (f32[1024,128]{1,0:T(8,128)}, f32[1024,128]{1,0:T(8,128)}) custom-call(bf16[32,16,128,128]{3,2,1,0:T(8,128)(2,1)} %bitcast.9, s32[16,32]{1,0:T(8,128)} %bitcast.11, s32[16,32]{1,0:T(8,128)} %bitcast.12, s32[1,32]{1,0:T(1,128)} %bitcast.13, bf16[64,128]{1,0:T(8,128)(2,1)} %bitcast.10, f32[32,4,1024]{2,1,0:T(4,128)} %prior_hbm.1), custom_call_target="tpu_custom_call" | custom-call | tf_op jit(solution)/shard_map/tomography/pallas_call | solution.py:583
  78.9 2.0 %reshape.10 = f32[32,4,1024]{2,1,0:T(4,128)} reshape(f32[1024,128]{1,0:T(8,128)} %get-tuple-element.4) | data formatting | bytes 1048576 | tf_op jit(solution)/shard_map/reshape | solution.py:640
  80.9 2.0 %reshape.11 = f32[32,4,1024]{2,1,0:T(4,128)} reshape(f32[1024,128]{1,0:T(8,128)} %get-tuple-element.5) | data formatting | bytes 1048576 | tf_op jit(solution)/shard_map/reshape | solution.py:640

commit v3 on v2

--- a/solution.py
+++ b/solution.py
@@ -543,18 +543,21 @@
     ratio = norm_1 / norm_0
     step_1 = norm_1 / (square + ratio * (cross + ratio * bend_0))
 
+    def as_field(x):
+        return x.T.reshape(levels, columns, runs * lanes)
+
     for turn in range(2):
         for copy in field_copies(turn):
             copy.wait_recv()
     start, later = shared[0].astype(F32), shared[1].astype(F32)
-    solution_ref[...] = (step_0 * start + step_1 * (later + ratio * start)).T
+    solution_ref[...] = as_field(step_0 * start + step_1 * (later + ratio * start))
     curved = place(5, 2) + prior_keep[1] + ratio * curved_keep[...]
     shared[2, quarter] = (own[1] - step_1 * curved).astype(BF16)
     for copy in field_copies(2):
         copy.start()
     for copy in field_copies(2):
         copy.wait_recv()
-    residual_ref[...] = shared[2].astype(F32).T
+    residual_ref[...] = as_field(shared[2].astype(F32))
 
     await_ids(x_send)
     for phase, buffer in ((1, 0), (3, 1), (5, 2)):
@@ -572,6 +575,23 @@
             copy.wait_send()
 
 
+def hand_over(solution_in, residual_in, solution_out, residual_out, kept, sem):
+    part = solution_in.shape[0] // 2
+    incoming, outgoing = [], []
+    for n, (src, dst) in enumerate(((solution_in, solution_out), (residual_in, residual_out))):
+        for k in range(2):
+            at = pl.ds(k * part, part)
+            incoming.append(pltpu.make_async_copy(src.at[at], kept.at[n, at], sem.at[0, 2 * n + k]))
+            outgoing.append(pltpu.make_async_copy(kept.at[n, at], dst.at[at], sem.at[1, 2 * n + k]))
+    for copy in incoming:
+        copy.start()
+    for arrives, leaves in zip(incoming, outgoing):
+        arrives.wait()
+        leaves.start()
+    for copy in outgoing:
+        copy.wait()
+
+
 def on_device(weights, slot_block, slot_tile, slot_count, observed, prior_scale):
     n_vox, n_ray = lax.axis_size("vox"), lax.axis_size("ray")
     n_dev = n_vox * n_ray
@@ -582,7 +602,7 @@
     vmem = pl.BlockSpec(memory_space=pltpu.VMEM)
     outs = pl.pallas_call(
         functools.partial(kernel, n_vox, n_ray, (levels, columns, runs, lanes)),
-        out_shape=[jax.ShapeDtypeStruct((blocks, lanes), F32)] * 2,
+        out_shape=[jax.ShapeDtypeStruct(prior_scale.shape, F32)] * 2,
         in_specs=[pl.BlockSpec(memory_space=pltpu.HBM)] * 6,
         out_specs=[vmem, vmem],
         scratch_shapes=[
@@ -637,7 +657,21 @@
         observed[:, 0],
         prior_scale,
     )
-    return tuple(out.reshape(levels, columns, across) for out in outs)
+    in_hbm = pl.BlockSpec(memory_space=pltpu.HBM)
+    return tuple(
+        pl.pallas_call(
+            hand_over,
+            out_shape=[jax.ShapeDtypeStruct(prior_scale.shape, F32)] * 2,
+            in_specs=[in_hbm] * 2,
+            out_specs=[in_hbm] * 2,
+            scratch_shapes=[
+                pltpu.VMEM((2,) + prior_scale.shape, F32),
+                pltpu.SemaphoreType.DMA((2, 4)),
+            ],
+            compiler_params=pltpu.CompilerParams(vmem_limit_bytes=64 * 2**20),
+            name="hand_over",
+        )(*outs)
+    )
 
 
 def solution(mesh):

time: 83.1 us -> 81.2 us (0.977)
  local copies, waits for them, and re-layouts: 4.01 us -> 0 us
  Pallas kernels: 78.3 us -> 80.3 us
    reshape x2 -> x0, local copies, waits for them, and re-layouts: 4.01 us -> none  [on_device(): return tuple((out.reshape(levels, columns, across) for out in outs))]
    pallas_call x0 -> x1, Pallas kernels: none -> 1.98 us  [on_device(): pl.pallas_call(hand_over, out_shape=[jax.ShapeDtypeStruct(prior_scale.sha...]
where the time goes in v3:
time: 81.2 us; the launch traced here: 81.1 us
  Pallas kernels  80.3 us (99%)
    pallas_call x1, Pallas kernels, on_device(): pl.pallas_call(functools.partial(kernel, n_vox, n_ray, (levels, columns,...  78.3 us
    pallas_call x1, Pallas kernels, on_device(): pl.pallas_call(hand_over, out_shape=[jax.ShapeDtypeStruct(prior_scale.sha...  1.98 us

profile of v3, /device:TPU:1, one launch (start us, length us, event | category | flops | bytes accessed | tf_op | source)
XLA Modules:
  0.0 81.1 jit_solution(12273465814403285372)
XLA Ops:
  0.6 78.3 %tomography.1 = (f32[32,4,1024]{2,1,0:T(4,128)}, f32[32,4,1024]{2,1,0:T(4,128)}) custom-call(bf16[32,16,128,128]{3,2,1,0:T(8,128)(2,1)} %bitcast.9, s32[16,32]{1,0:T(8,128)} %bitcast.11, s32[16,32]{1,0:T(8,128)} %bitcast.12, s32[1,32]{1,0:T(1,128)} %bitcast.13, bf16[64,128]{1,0:T(8,128)(2,1)} %bitcast.10, f32[32,4,1024]{2,1,0:T(4,128)} %prior_hbm.1), custom_call_target="tpu_custom_call" | custom-call | tf_op jit(solution)/shard_map/tomography/pallas_call | solution.py:603
  78.9 2.0 %hand_over.1 = (f32[32,4,1024]{2,1,0:T(4,128)}, f32[32,4,1024]{2,1,0:T(4,128)}) custom-call(f32[32,4,1024]{2,1,0:T(4,128)} %get-tuple-element.4.solution_in, f32[32,4,1024]{2,1,0:T(4,128)} %get-tuple-element.5.residual_in), custom_call_target="tpu_custom_call" | custom-call | tf_op jit(solution)/shard_map/hand_over/pallas_call | solution.py:662
